TPU v7x, 256 devices: a whole 4x4x8 slice. The times are simulated.
256 devices in a mesh: paper: 32 (over x_lo, z, core), type: 8 (over y, x_hi).
Axes of the slice: x: 4 (x_hi: 2, x_lo: 2; x = x_hi * 2 + x_lo), y: 4, z: 8, core: 2. Of those that a mesh axis runs over, the one named last changes fastest.
Arguments:
- papers: bfloat16 [131072, 512], P(('paper', 'type')), may hold values from -6 to 6
- cited_rows: bfloat16 [4096, 512], P('paper'), may hold values from -6 to 6
- entities: bfloat16 [1024, 512], P('type'), may hold values from -6 to 6
- entity_kinds: int32 [1024], P('type'), may hold values from 0 to 1
- query_weight: bfloat16 [512, 512], replicated, may hold values from -0.25 to 0.25
- key_weight: bfloat16 [3, 512, 512], replicated, may hold values from -0.25 to 0.25
- value_weight: bfloat16 [3, 512, 512], replicated, may hold values from -0.25 to 0.25
- attention_rel: bfloat16 [4, 8, 64, 64], replicated, may hold values from -0.75 to 0.75
- message_rel: bfloat16 [4, 8, 64, 64], replicated, may hold values from -0.75 to 0.75
- relation_prior: float32 [4, 8], replicated, may hold values from 0.5 to 2.5
- output_weight: bfloat16 [512, 512], replicated, may hold values from -0.25 to 0.25
- skip_gate: float32 [1], replicated, may hold values from -1 to 1
- norm_gain: float32 [512], replicated, may hold values from 0.5 to 1.5
- cite_pattern: int32 [1024, 8, 128, 128], P(('paper', 'type')), may hold values from 0 to 1, as said below
- cite_tiles: int32 [1024, 8], P(('paper', 'type')), may hold values from 0 to 31, as said below
- cite_counts: int32 [1024, 8], P(('paper', 'type')), may hold values from 0 to 16384, as said below
- entity_pattern: int32 [1024, 2, 128, 128], P(('paper', 'type')), may hold values from 0 to 1, as said below
- entity_tiles: int32 [1024, 2], P(('paper', 'type')), may hold values from 0 to 7, as said below
- entity_counts: int32 [1024, 2], P(('paper', 'type')), may hold values from 0 to 16384, as said below
Outputs:
- updated: bfloat16 [131072, 512], P(('paper', 'type'))
Inputs may be any that keep to these rules, and one draw needn't show every extreme that they name: `cite_pattern`: entry [a, k, p, c] is 1 where paper 128 * a + p has an edge from source 128 * cite_tiles[a, k] + c, else 0. A tile of papers uses its first 8, 4, 2 or 1 slots (at least one), the same number for all tiles of one device's papers; later slots are all zero. `cite_tiles`: the slots of one tile name distinct tiles. `cite_counts`: the number of ones in the slot's block. `entity_pattern`: as cite_pattern, with sources 128 * entity_tiles[a, k] + c; a tile uses its first 1 to 2 slots, later slots are all zero. `entity_tiles`: the slots of one tile name distinct tiles. `entity_counts`: the number of ones in the slot's block.
All inputs are finite; a program needn't handle non-finite values.
Results may differ from a plain program's by a relative error of at most 0.0087.
Values may be sent and summed in bfloat16 or wider, within the bound.
No kernel may reach another device: no remote copies, remote signals or barrier semaphores. Data moves between devices by JAX's collectives and lax.ppermute only.
A program may use at most 128 MiB of HBM per device.

v0:
```python
import math
import jax
import jax.numpy as jnp
from jax import lax
from jax.sharding import PartitionSpec as P

CAP = 20.0


def head_split(matrix, head_count):
    return matrix.reshape(matrix.shape[0], head_count, matrix.shape[1] // head_count)


def relate(raw_rows, weight):
    head_count = weight.shape[0]
    mapped = jnp.einsum(
        "nhd,hde->nhe", head_split(raw_rows, head_count), weight, preferred_element_type=jnp.float32
    )
    return mapped.reshape(raw_rows.shape)


def project(source_rows, weight):
    return jnp.dot(source_rows, weight, preferred_element_type=jnp.float32).astype(jnp.bfloat16)


def cited_pairs(source_rows, key_weight, value_weight, attention_rel, message_rel):
    key_rows = relate(project(source_rows, key_weight[0]), attention_rel[0]).astype(jnp.bfloat16)
    value_rows = relate(project(source_rows, value_weight[0]), message_rel[0]).astype(jnp.bfloat16)
    return (key_rows, value_rows)


def entity_side(source_rows, kind_ids, key_weight, value_weight, attention_rel, message_rel):
    author = (kind_ids == 0)[:, None]
    key_raw = jnp.where(
        author,
        jnp.dot(source_rows, key_weight[1], preferred_element_type=jnp.float32),
        jnp.dot(source_rows, key_weight[2], preferred_element_type=jnp.float32),
    ).astype(jnp.bfloat16)
    value_raw = jnp.where(
        author,
        jnp.dot(source_rows, value_weight[1], preferred_element_type=jnp.float32),
        jnp.dot(source_rows, value_weight[2], preferred_element_type=jnp.float32),
    ).astype(jnp.bfloat16)
    key_rows = jnp.where(
        author, relate(key_raw, attention_rel[1]), relate(key_raw, attention_rel[2])
    ).astype(jnp.bfloat16)
    value_rows = jnp.where(
        author, relate(value_raw, message_rel[1]), relate(value_raw, message_rel[2])
    ).astype(jnp.bfloat16)
    return (key_rows, value_rows)


def kind_scales(kind_ids, relation_prior, inv_root):
    author = (kind_ids == 0)[:, None]
    return jnp.where(author, relation_prior[1][None, :], relation_prior[2][None, :]) * inv_root


def own_term(query_heads, own_key, own_value, scale):
    head_count = query_heads.shape[1]
    own_dot = jnp.sum(
        query_heads.astype(jnp.float32) * head_split(own_key, head_count).astype(jnp.float32),
        axis=2,
    )
    weights = jnp.exp(CAP * jnp.tanh(own_dot * scale / CAP))
    rounded = lax.optimization_barrier(weights.astype(jnp.bfloat16)).astype(jnp.float32)
    return (rounded[:, :, None] * head_split(own_value, head_count).astype(jnp.float32), weights)


def dense_live(pattern, tile_ids, counts, source_count):
    chosen = (tile_ids[:, :, None] == jnp.arange(source_count, dtype=jnp.int32)[None, None, :]) & (
        counts[:, :, None] > 0
    )
    spread = jnp.einsum(
        "ikj,ikac->iajc",
        chosen.astype(jnp.bfloat16),
        pattern.astype(jnp.bfloat16),
        preferred_element_type=jnp.float32,
    )
    return (
        spread.reshape(pattern.shape[0] * pattern.shape[2], source_count * pattern.shape[3]) > 0.5
    )


def attend(running, query_heads, key_rows, value_rows, scales, live_mask):
    head_count = query_heads.shape[1]
    products = jnp.einsum(
        "thd,shd->hts",
        query_heads,
        head_split(key_rows, head_count),
        preferred_element_type=jnp.float32,
    )
    scores = products * scales.T[:, None, :]
    scores = CAP * jnp.tanh(scores / CAP)
    weights = jnp.where(live_mask[None, :, :], jnp.exp(scores), 0.0)
    numerator, denominator = running
    numerator = numerator + jnp.einsum(
        "hts,shd->thd",
        weights.astype(jnp.bfloat16),
        head_split(value_rows, head_count),
        preferred_element_type=jnp.float32,
    )
    denominator = denominator + jnp.sum(weights, axis=2).T
    return (numerator, denominator)


def sweep_dense(running, query_heads, key_rows, value_rows, scales, live_mask):
    row_count = key_rows.shape[0]
    block_rows = math.gcd(row_count, 512)
    block_count = row_count // block_rows

    def single_block(offset, state):
        part_keys = lax.dynamic_slice_in_dim(key_rows, offset, block_rows, 0)
        part_values = lax.dynamic_slice_in_dim(value_rows, offset, block_rows, 0)
        part_scales = lax.dynamic_slice_in_dim(scales, offset, block_rows, 0)
        part_live = lax.dynamic_slice_in_dim(live_mask, offset, block_rows, 1)
        return attend(state, query_heads, part_keys, part_values, part_scales, part_live)

    return lax.fori_loop(
        0, block_count, lambda position, state: single_block(position * block_rows, state), running
    )


def per_device(
    papers,
    cited_rows,
    entities,
    entity_kinds,
    query_weight,
    key_weight,
    value_weight,
    attention_rel,
    message_rel,
    relation_prior,
    output_weight,
    skip_gate,
    norm_gain,
    cite_pattern,
    cite_tiles,
    cite_counts,
    entity_pattern,
    entity_tiles,
    entity_counts,
):
    head_count = relation_prior.shape[1]
    model_width = papers.shape[1]
    inv_root = 1.0 / math.sqrt(model_width // head_count)
    tile_size = cite_pattern.shape[2]
    query_heads = head_split(project(papers, query_weight), head_count)
    own_keys = relate(project(papers, key_weight[0]), attention_rel[3]).astype(jnp.bfloat16)
    own_values = relate(project(papers, value_weight[0]), message_rel[3]).astype(jnp.bfloat16)
    running = own_term(query_heads, own_keys, own_values, relation_prior[3] * inv_root)
    cite_sources = cited_rows.shape[0] * lax.axis_size("paper") // tile_size
    entity_sources = entities.shape[0] * lax.axis_size("type") // tile_size
    cite_live = dense_live(cite_pattern, cite_tiles, cite_counts, cite_sources)
    entity_live = dense_live(entity_pattern, entity_tiles, entity_counts, entity_sources)
    cite_scale = relation_prior[0] * inv_root

    def sweep_rows(state, key_rows, value_rows, scales, live_mask):
        return sweep_dense(state, query_heads, key_rows, value_rows, scales, live_mask)

    cite_keys, cite_values = cited_pairs(
        cited_rows, key_weight, value_weight, attention_rel, message_rel
    )
    key_rows = lax.all_gather(cite_keys, "paper", axis=0, tiled=True)
    value_rows = lax.all_gather(cite_values, "paper", axis=0, tiled=True)
    row_count = key_rows.shape[0]
    scales = jnp.broadcast_to(cite_scale[None, :], (row_count, head_count))
    live_mask = cite_live
    running = sweep_rows(running, key_rows, value_rows, scales, live_mask)
    entity_keys, entity_values = entity_side(
        entities, entity_kinds, key_weight, value_weight, attention_rel, message_rel
    )
    key_rows = lax.all_gather(entity_keys, "type", axis=0, tiled=True)
    value_rows = lax.all_gather(entity_values, "type", axis=0, tiled=True)
    kind_ids = lax.all_gather(entity_kinds, "type", axis=0, tiled=True)
    live_mask = entity_live
    scales = kind_scales(kind_ids, relation_prior, inv_root)
    running = sweep_rows(running, key_rows, value_rows, scales, live_mask)
    numerator, denominator = running
    mixed = numerator / denominator[:, :, None]
    hidden = jax.nn.gelu(mixed, approximate=False).reshape(papers.shape).astype(jnp.bfloat16)
    projected = jnp.dot(hidden, output_weight, preferred_element_type=jnp.float32)
    alpha = jax.nn.sigmoid(skip_gate[0])
    blended = alpha * projected + (1.0 - alpha) * papers.astype(jnp.float32)
    centre = jnp.mean(blended, axis=1, keepdims=True)
    spread = jnp.mean(jnp.square(blended - centre), axis=1, keepdims=True)
    return ((blended - centre) * lax.rsqrt(spread + 1e-05) * norm_gain).astype(jnp.bfloat16)


def solution(mesh):
    in_specs = (
        P(("paper", "type"), None),
        P("paper", None),
        P("type", None),
        P("type"),
        P(),
        P(),
        P(),
        P(),
        P(),
        P(),
        P(),
        P(),
        P(),
        P(("paper", "type"), None, None, None),
        P(("paper", "type"), None),
        P(("paper", "type"), None),
        P(("paper", "type"), None, None, None),
        P(("paper", "type"), None),
        P(("paper", "type"), None),
    )
    out_specs = P(("paper", "type"), None)
    return jax.shard_map(
        per_device, mesh=mesh, in_specs=in_specs, out_specs=out_specs, check_vma=False
    )
```

profile of v0, /device:TPU:32, one launch (start us, length us, event | category | flops | bytes accessed | tf_op | source)
XLA Modules:
  0.0 305.5 jit_solution(12606027069432902656)
XLA Ops:
  29.2 2.3 convolution_convert_fusion.3
  31.5 2.4 convolution_convert_fusion.2
  39.2 2.5 broadcast_compare_fusion
  41.7 3.0 copy.131
  44.7 23.5 %all-gather = s32[8,1,128]{2,1,0:T(1,128)S(1)} all-gather(s32[1,1,128]{2,1,0:T(1,128)S(1)} %bitcast.259), channel_id=1, replica_groups=mesh['paper'=32,'type'=8] {'type'}, dimensions={0}, use_global_device_ids=true | all-gather | bytes 4608 | tf_op jit(solution)/shard_map/all_gather | solution.py:175
  70.2 2.3 fusion.34
  72.5 12.5 %all-gather.6.cloned.1.call-done = bf16[4096,512]{0,1:T(8,128)(2,1)} async-done(((bf16[128,512]{0,1:T(8,128)(2,1)}), bf16[4096,512]{0,1:T(8,128)(2,1)}) %all-gather.6.cloned.1.call-update) | async-done | bytes 4194320 | tf_op jit(solution)/shard_map/all_gather | solution.py:165
  85.0 72.5 %all-gather.8.cloned.1.call-done = bf16[4096,512]{0,1:T(8,128)(2,1)} async-done(((bf16[128,512]{0,1:T(8,128)(2,1)}), bf16[4096,512]{0,1:T(8,128)(2,1)}) %all-gather.8.cloned.1.call-update) | async-done | bytes 4194320 | tf_op jit(solution)/shard_map/all_gather | solution.py:164
  158.3 92.3 %while.30 = (s32[]{:T(128)}, f32[512,8,64]{0,2,1:T(8,128)}, f32[512,8]{0,1:T(8,128)S(1)}, bf16[4096,512]{0,1:T(8,128)(2,1)}, pred[512,4096]{1,0:T(8,128)(4,1)}, ...) while((s32[]{:T(128)}, f32[512,8,64]{0,2,1:T(8,128)}, ...), condition=%wide.region_3.4_spmd, body=%wide.region_1.3_spmd.sunk | while | flops 558104576 | bytes 32637160 | solution.py:118
  161.6 4.5 %fusion.143 = (f32[8,512]{1,0:T(8,128)S(1)}, f32[8,512,512]{2,1,0:T(8,128)S(1)}) fusion(f32[8,512]{1,0:T(8,128)S(1)} %dynamic-slice_bitcast_fusion.4, pred[512,512]{0,1:T(8,128)(4,1)S(1)} %copy.137, bf16[512,8,64]{0,2,1:T(8,128)(2,1)S(1)} %bitcast.234, bf16[512,8,64]{0,2,1:T(8,128)(2,1)} %get-tuple-element.531), kind=kOutput, calls=%fused_computation.1.clone.1 | convolution fusion | flops 278917120 | bytes 9732096 | tf_op jit(solution)/shard_map/while/body/eval_jaxpr/thd,shd->hts/dot_general | solution.py:86
  166.1 2.6 fusion.144
  173.2 4.5 %fusion.143 = (f32[8,512]{1,0:T(8,128)S(1)}, f32[8,512,512]{2,1,0:T(8,128)S(1)}) fusion(f32[8,512]{1,0:T(8,128)S(1)} %dynamic-slice_bitcast_fusion.4, pred[512,512]{0,1:T(8,128)(4,1)S(1)} %copy.137, bf16[512,8,64]{0,2,1:T(8,128)(2,1)S(1)} %bitcast.234, bf16[512,8,64]{0,2,1:T(8,128)(2,1)} %get-tuple-element.531), kind=kOutput, calls=%fused_computation.1.clone.1 | convolution fusion | flops 278917120 | bytes 9732096 | tf_op jit(solution)/shard_map/while/body/eval_jaxpr/thd,shd->hts/dot_general | solution.py:86
  177.7 2.6 fusion.144
  184.8 4.5 %fusion.143 = (f32[8,512]{1,0:T(8,128)S(1)}, f32[8,512,512]{2,1,0:T(8,128)S(1)}) fusion(f32[8,512]{1,0:T(8,128)S(1)} %dynamic-slice_bitcast_fusion.4, pred[512,512]{0,1:T(8,128)(4,1)S(1)} %copy.137, bf16[512,8,64]{0,2,1:T(8,128)(2,1)S(1)} %bitcast.234, bf16[512,8,64]{0,2,1:T(8,128)(2,1)} %get-tuple-element.531), kind=kOutput, calls=%fused_computation.1.clone.1 | convolution fusion | flops 278917120 | bytes 9732096 | tf_op jit(solution)/shard_map/while/body/eval_jaxpr/thd,shd->hts/dot_general | solution.py:86
  189.2 2.6 fusion.144
  196.3 4.5 %fusion.143 = (f32[8,512]{1,0:T(8,128)S(1)}, f32[8,512,512]{2,1,0:T(8,128)S(1)}) fusion(f32[8,512]{1,0:T(8,128)S(1)} %dynamic-slice_bitcast_fusion.4, pred[512,512]{0,1:T(8,128)(4,1)S(1)} %copy.137, bf16[512,8,64]{0,2,1:T(8,128)(2,1)S(1)} %bitcast.234, bf16[512,8,64]{0,2,1:T(8,128)(2,1)} %get-tuple-element.531), kind=kOutput, calls=%fused_computation.1.clone.1 | convolution fusion | flops 278917120 | bytes 9732096 | tf_op jit(solution)/shard_map/while/body/eval_jaxpr/thd,shd->hts/dot_general | solution.py:86
  200.8 2.6 fusion.144
  207.8 4.5 %fusion.143 = (f32[8,512]{1,0:T(8,128)S(1)}, f32[8,512,512]{2,1,0:T(8,128)S(1)}) fusion(f32[8,512]{1,0:T(8,128)S(1)} %dynamic-slice_bitcast_fusion.4, pred[512,512]{0,1:T(8,128)(4,1)S(1)} %copy.137, bf16[512,8,64]{0,2,1:T(8,128)(2,1)S(1)} %bitcast.234, bf16[512,8,64]{0,2,1:T(8,128)(2,1)} %get-tuple-element.531), kind=kOutput, calls=%fused_computation.1.clone.1 | convolution fusion | flops 278917120 | bytes 9732096 | tf_op jit(solution)/shard_map/while/body/eval_jaxpr/thd,shd->hts/dot_general | solution.py:86
  212.3 2.6 fusion.144
  219.4 4.5 %fusion.143 = (f32[8,512]{1,0:T(8,128)S(1)}, f32[8,512,512]{2,1,0:T(8,128)S(1)}) fusion(f32[8,512]{1,0:T(8,128)S(1)} %dynamic-slice_bitcast_fusion.4, pred[512,512]{0,1:T(8,128)(4,1)S(1)} %copy.137, bf16[512,8,64]{0,2,1:T(8,128)(2,1)S(1)} %bitcast.234, bf16[512,8,64]{0,2,1:T(8,128)(2,1)} %get-tuple-element.531), kind=kOutput, calls=%fused_computation.1.clone.1 | convolution fusion | flops 278917120 | bytes 9732096 | tf_op jit(solution)/shard_map/while/body/eval_jaxpr/thd,shd->hts/dot_general | solution.py:86
  223.8 2.6 fusion.144
  230.9 4.5 %fusion.143 = (f32[8,512]{1,0:T(8,128)S(1)}, f32[8,512,512]{2,1,0:T(8,128)S(1)}) fusion(f32[8,512]{1,0:T(8,128)S(1)} %dynamic-slice_bitcast_fusion.4, pred[512,512]{0,1:T(8,128)(4,1)S(1)} %copy.137, bf16[512,8,64]{0,2,1:T(8,128)(2,1)S(1)} %bitcast.234, bf16[512,8,64]{0,2,1:T(8,128)(2,1)} %get-tuple-element.531), kind=kOutput, calls=%fused_computation.1.clone.1 | convolution fusion | flops 278917120 | bytes 9732096 | tf_op jit(solution)/shard_map/while/body/eval_jaxpr/thd,shd->hts/dot_general | solution.py:86
  235.4 2.6 fusion.144
  242.4 4.5 %fusion.143 = (f32[8,512]{1,0:T(8,128)S(1)}, f32[8,512,512]{2,1,0:T(8,128)S(1)}) fusion(f32[8,512]{1,0:T(8,128)S(1)} %dynamic-slice_bitcast_fusion.4, pred[512,512]{0,1:T(8,128)(4,1)S(1)} %copy.137, bf16[512,8,64]{0,2,1:T(8,128)(2,1)S(1)} %bitcast.234, bf16[512,8,64]{0,2,1:T(8,128)(2,1)} %get-tuple-element.531), kind=kOutput, calls=%fused_computation.1.clone.1 | convolution fusion | flops 278917120 | bytes 9732096 | tf_op jit(solution)/shard_map/while/body/eval_jaxpr/thd,shd->hts/dot_general | solution.py:86
  246.9 2.6 fusion.144
  250.6 12.6 %all-gather.12.cloned.1.call-done = bf16[1024,512]{1,0:T(8,128)(2,1)} async-done(((bf16[128,512]{1,0:T(8,128)(2,1)}), bf16[1024,512]{1,0:T(8,128)(2,1)}) %all-gather.12.cloned.1.call-update) | async-done | bytes 1048592 | tf_op jit(solution)/shard_map/all_gather | solution.py:173
  263.2 29.5 %while.31 = (s32[]{:T(128)}, f32[512,8,64]{0,2,1:T(8,128)}, f32[512,8]{0,1:T(8,128)S(1)}, bf16[1024,512]{1,0:T(8,128)(2,1)}, pred[512,1024]{1,0:T(8,128)(4,1)S(1...) while((s32[]{:T(128)}, f32[512,8,64]{0,2,1:T(8,128)}, ...), condition=%wide.region_6.7_spmd, body=%wide.region_4.6_spmd.sunk | while | flops 558104576 | bytes 34734312 | solution.py:118
  265.1 6.5 %fusion.149 = (f32[8,512]{1,0:T(8,128)S(1)}, f32[8,512,512]{2,1,0:T(8,128)}) fusion(f32[8,512]{1,0:T(8,128)S(1)} %dynamic-slice_bitcast_fusion.5, pred[512,512]{0,1:T(8,128)(4,1)S(1)} %copy.139, bf16[512,8,64]{0,2,1:T(8,128)(2,1)S(1)} %bitcast.235, bf16[512,8,64]{0,2,1:T(8,128)(2,1)} %get-tuple-element.567), kind=kOutput, calls=%fused_computation.16.clone.1 | convolution fusion | flops 278917120 | bytes 9732096 | tf_op jit(solution)/shard_map/while/body/eval_jaxpr/thd,shd->hts/dot_general | solution.py:86
  271.8 5.0 %fusion.150 = f32[512,8,64]{0,2,1:T(8,128)S(1)} fusion(f32[512,8,64]{0,2,1:T(8,128)S(1)} %copy-done.3, bf16[512,8,64]{0,2,1:T(8,128)(2,1)S(1)} %bitcast.236, f32[8,512,512]{2,1,0:T(8,128)} %get-tuple-element.499, f32[8,512]{1,0:T(8,128)S(1)} %dynamic-slice_bitcast_fusion.5, pred[512,512]{0,1:T(8,128)(4,1)S(1)} %copy.139), kind=kOutput, calls=%fused_computation.21.clone.1 | convolution fusion | flops 279183360 | bytes 11288576 | tf_op jit(solution)/shard_map/while/body/eval_jaxpr/hts,shd->thd/dot_general | solution.py:96
  279.9 6.5 %fusion.149 = (f32[8,512]{1,0:T(8,128)S(1)}, f32[8,512,512]{2,1,0:T(8,128)}) fusion(f32[8,512]{1,0:T(8,128)S(1)} %dynamic-slice_bitcast_fusion.5, pred[512,512]{0,1:T(8,128)(4,1)S(1)} %copy.139, bf16[512,8,64]{0,2,1:T(8,128)(2,1)S(1)} %bitcast.235, bf16[512,8,64]{0,2,1:T(8,128)(2,1)} %get-tuple-element.567), kind=kOutput, calls=%fused_computation.16.clone.1 | convolution fusion | flops 278917120 | bytes 9732096 | tf_op jit(solution)/shard_map/while/body/eval_jaxpr/thd,shd->hts/dot_general | solution.py:86
  286.6 5.0 %fusion.150 = f32[512,8,64]{0,2,1:T(8,128)S(1)} fusion(f32[512,8,64]{0,2,1:T(8,128)S(1)} %copy-done.3, bf16[512,8,64]{0,2,1:T(8,128)(2,1)S(1)} %bitcast.236, f32[8,512,512]{2,1,0:T(8,128)} %get-tuple-element.499, f32[8,512]{1,0:T(8,128)S(1)} %dynamic-slice_bitcast_fusion.5, pred[512,512]{0,1:T(8,128)(4,1)S(1)} %copy.139), kind=kOutput, calls=%fused_computation.21.clone.1 | convolution fusion | flops 279183360 | bytes 11288576 | tf_op jit(solution)/shard_map/while/body/eval_jaxpr/hts,shd->thd/dot_general | solution.py:96
  292.6 3.4 %fusion.40 = bf16[512,8,64]{0,2,1:T(8,128)(2,1)S(1)} fusion(f32[512,8,64]{0,2,1:T(8,128)} %get-tuple-element.287, f32[512,8]{0,1:T(8,128)S(1)} %get-tuple-element.288), kind=kLoop, calls=%fused_computation.59 | loop fusion | flops 17301504 | bytes 1589248 | tf_op jit(solution)/shard_map/convert_element_type | solution.py:181
  (170 shorter events, 74.1 us)
Async XLA Ops:
  6.5 289.5 %copy-start = (bf16[512,512]{1,0:T(8,128)(2,1)S(1)}, bf16[512,512]{1,0:T(8,128)(2,1)}, u32[]{:S(2)}) copy-start(bf16[512,512]{1,0:T(8,128)(2,1)} %param.33) | copy-start | bytes 1572868
  6.5 22.7 %copy-start.6 = (bf16[512,512]{1,0:T(8,128)(2,1)S(1)}, bf16[512,512]{1,0:T(8,128)(2,1)}, u32[]{:S(2)}) copy-start(bf16[512,512]{1,0:T(8,128)(2,1)} %param.23) | copy-start | bytes 1572868
  6.5 28.4 %copy-start.11 = (f32[4,8]{1,0:T(4,128)S(1)}, f32[4,8]{1,0:T(4,128)}, u32[]{:S(2)}) copy-start(f32[4,8]{1,0:T(4,128)} %param.32) | copy-start | bytes 388
  6.5 78.5 %all-gather.6.cloned.1.call-start = ((), (), s32[]{:S(2)}) async-start(), calls=%async_computation | async-start | bytes 4325376 | tf_op jit(solution)/shard_map/all_gather | solution.py:165
  9.9 28.3 %copy-start.7 = (s32[4,8,128,128]{3,2,1,0:T(8,128)S(1)}, s32[4,8,128,128]{3,2,1,0:T(8,128)}, u32[]{:S(2)}) copy-start(s32[4,8,128,128]{3,2,1,0:T(8,128)} %param.36) | copy-start | bytes 6291460
  9.9 147.6 %all-gather.8.cloned.1.call-start = ((), (), s32[]{:S(2)}) async-start(), calls=%async_computation.1 | async-start | bytes 4325376 | tf_op jit(solution)/shard_map/all_gather | solution.py:164
  13.4 237.2 %all-gather.10.cloned.1.call-start = ((), (), s32[]{:S(2)}) async-start(), calls=%async_computation.2 | async-start | bytes 1179648 | tf_op jit(solution)/shard_map/all_gather | solution.py:174
  28.6 234.5 %all-gather.12.cloned.1.call-start = ((), (), s32[]{:S(2)}) async-start(), calls=%async_computation.3 | async-start | bytes 1179648 | tf_op jit(solution)/shard_map/all_gather | solution.py:173
  36.5 1.7 copy-start.5
  39.2 5.6 %copy-start.13 = (s32[128]{0:T(128)S(1)}, s32[128]{0:T(128)}, u32[]{:S(2)}) copy-start(s32[128]{0:T(128)} %param.26) | copy-start | bytes 1540
  39.2 29.0 %copy-start.8 = (s32[4,2,128,128]{3,2,1,0:T(8,128)S(1)}, s32[4,2,128,128]{3,2,1,0:T(8,128)}, u32[]{:S(2)}) copy-start(s32[4,2,128,128]{3,2,1,0:T(8,128)} %param.39) | copy-start | bytes 1572868
  39.2 29.1 %copy-start.12 = (s32[4,2]{0,1:T(2,128)S(1)}, s32[4,2]{0,1:T(2,128)}, u32[]{:S(2)}) copy-start(s32[4,2]{0,1:T(2,128)} %param.40) | copy-start | bytes 100
  39.2 29.2 %copy-start.14 = (s32[4,2]{0,1:T(2,128)S(1)}, s32[4,2]{0,1:T(2,128)}, u32[]{:S(2)}) copy-start(s32[4,2]{0,1:T(2,128)} %param.41) | copy-start | bytes 100
  41.7 28.5 %copy-start.9 = (bf16[512,512]{0,1:T(8,128)(2,1)S(1)}, bf16[512,512]{0,1:T(8,128)(2,1)}, u32[]{:S(2)}) copy-start(bf16[512,512]{0,1:T(8,128)(2,1)} %convolution_convert_fusion.2) | copy-start | bytes 1572868
  161.6 4.5 %copy-start.1 = (f32[512,8,64]{0,2,1:T(8,128)S(1)}, f32[512,8,64]{0,2,1:T(8,128)}, u32[]{:S(2)}) copy-start(f32[512,8,64]{0,2,1:T(8,128)} %get-tuple-element.514) | copy-start | bytes 3145732 | tf_op jit(solution)/shard_map/while
  168.8 1.0 copy-start.2
  173.2 4.5 %copy-start.1 = (f32[512,8,64]{0,2,1:T(8,128)S(1)}, f32[512,8,64]{0,2,1:T(8,128)}, u32[]{:S(2)}) copy-start(f32[512,8,64]{0,2,1:T(8,128)} %get-tuple-element.514) | copy-start | bytes 3145732 | tf_op jit(solution)/shard_map/while
  180.3 1.0 copy-start.2
  184.8 4.5 %copy-start.1 = (f32[512,8,64]{0,2,1:T(8,128)S(1)}, f32[512,8,64]{0,2,1:T(8,128)}, u32[]{:S(2)}) copy-start(f32[512,8,64]{0,2,1:T(8,128)} %get-tuple-element.514) | copy-start | bytes 3145732 | tf_op jit(solution)/shard_map/while
  191.9 1.0 copy-start.2
  196.3 4.5 %copy-start.1 = (f32[512,8,64]{0,2,1:T(8,128)S(1)}, f32[512,8,64]{0,2,1:T(8,128)}, u32[]{:S(2)}) copy-start(f32[512,8,64]{0,2,1:T(8,128)} %get-tuple-element.514) | copy-start | bytes 3145732 | tf_op jit(solution)/shard_map/while
  203.4 1.0 copy-start.2
  207.8 4.5 %copy-start.1 = (f32[512,8,64]{0,2,1:T(8,128)S(1)}, f32[512,8,64]{0,2,1:T(8,128)}, u32[]{:S(2)}) copy-start(f32[512,8,64]{0,2,1:T(8,128)} %get-tuple-element.514) | copy-start | bytes 3145732 | tf_op jit(solution)/shard_map/while
  215.0 1.0 copy-start.2
  219.4 4.5 %copy-start.1 = (f32[512,8,64]{0,2,1:T(8,128)S(1)}, f32[512,8,64]{0,2,1:T(8,128)}, u32[]{:S(2)}) copy-start(f32[512,8,64]{0,2,1:T(8,128)} %get-tuple-element.514) | copy-start | bytes 3145732 | tf_op jit(solution)/shard_map/while
  226.5 1.0 copy-start.2
  230.9 4.5 %copy-start.1 = (f32[512,8,64]{0,2,1:T(8,128)S(1)}, f32[512,8,64]{0,2,1:T(8,128)}, u32[]{:S(2)}) copy-start(f32[512,8,64]{0,2,1:T(8,128)} %get-tuple-element.514) | copy-start | bytes 3145732 | tf_op jit(solution)/shard_map/while
  238.0 1.0 copy-start.2
  242.4 4.5 %copy-start.1 = (f32[512,8,64]{0,2,1:T(8,128)S(1)}, f32[512,8,64]{0,2,1:T(8,128)}, u32[]{:S(2)}) copy-start(f32[512,8,64]{0,2,1:T(8,128)} %get-tuple-element.514) | copy-start | bytes 3145732 | tf_op jit(solution)/shard_map/while
  263.2 34.7 %copy-start.10 = (f32[512]{0:T(512)S(1)}, f32[512]{0:T(512)}, u32[]{:S(2)}) copy-start(f32[512]{0:T(512)} %param.35) | copy-start | bytes 6148
  265.1 6.7 %copy-start.3 = (f32[512,8,64]{0,2,1:T(8,128)S(1)}, f32[512,8,64]{0,2,1:T(8,128)}, u32[]{:S(2)}) copy-start(f32[512,8,64]{0,2,1:T(8,128)} %get-tuple-element.550) | copy-start | bytes 3145732 | tf_op jit(solution)/shard_map/while
  279.8 6.7 %copy-start.3 = (f32[512,8,64]{0,2,1:T(8,128)S(1)}, f32[512,8,64]{0,2,1:T(8,128)}, u32[]{:S(2)}) copy-start(f32[512,8,64]{0,2,1:T(8,128)} %get-tuple-element.550) | copy-start | bytes 3145732 | tf_op jit(solution)/shard_map/while
  (3 other events, 3.1 us)
Sparse Core Ops, SparseCore 0:
  10.0 74.9 all-gather.5
  86.8 70.6 all-gather.7
  160.2 50.1 all-gather.9
  212.8 50.2 all-gather.11
where the time goes:
time: 307 us; the launch traced here: 306 us
  matrix products  111 us (36%)
  waiting for transfers between devices  98.1 us (32%)
  local copies, waits for them, and re-layouts  50.6 us (16%)
  blocking collectives  23.5 us (8%)
  between operations  14.1 us (5%)
  other arithmetic  7.42 us (2%)
    all_gather x1, waiting for transfers between devices, per_device(): key_rows = lax.all_gather(cite_keys, 'paper', axis=0, tiled=True)  72.5 us
    dot_general x10, matrix products, attend(): jnp.einsum('thd,shd->hts', query_heads, head_split(key_rows, head_count),...  48.6 us
    dot_general x10, matrix products, attend(): jnp.einsum('hts,shd->thd', weights.astype(jnp.bfloat16), head_split(value...  31.2 us
    all_gather x1, blocking collectives, per_device(): kind_ids = lax.all_gather(entity_kinds, 'type', axis=0, tiled=True)  23.5 us
    dynamic_slice x12, local copies, waits for them, and re-layouts, single_block(): part_keys = lax.dynamic_slice_in_dim(key_rows, offset, block_rows, 0)  13.2 us
    all_gather x1, waiting for transfers between devices, per_device(): key_rows = lax.all_gather(entity_keys, 'type', axis=0, tiled=True)  12.6 us
    all_gather x1, waiting for transfers between devices, per_device(): value_rows = lax.all_gather(cite_values, 'paper', axis=0, tiled=True)  12.5 us
    dot_general x8, matrix products, relate(): jnp.einsum('nhd,hde->nhe', head_split(raw_rows, head_count), weight, pref...  12 us
  transfers between devices with their start and end apart: 4, of which 3 were waited for; matrix products, arithmetic and copies ran while one was open for 40% of the time, Pallas kernels for 0%

commit v1 on v0

--- a/solution.py
+++ b/solution.py
@@ -162,7 +162,9 @@
         cited_rows, key_weight, value_weight, attention_rel, message_rel
     )
     key_rows = lax.all_gather(cite_keys, "paper", axis=0, tiled=True)
-    value_rows = lax.all_gather(cite_values, "paper", axis=0, tiled=True)
+    value_rows = jnp.concatenate(
+        lax.all_to_all(jnp.stack([cite_values] * lax.axis_size("paper")), "paper", 0, 0), axis=0
+    )
     row_count = key_rows.shape[0]
     scales = jnp.broadcast_to(cite_scale[None, :], (row_count, head_count))
     live_mask = cite_live

time: 307 us -> 320 us (1.042)
  waiting for transfers between devices: 98.1 us -> 67 us
  matrix products: 111 us -> 136 us
  starting transfers between devices: 0.13 us -> 9.93 us
  local copies, waits for them, and re-layouts: 50.6 us -> 58.6 us
    all_gather x1, waiting for transfers between devices: 72.5 us -> 0.01 us  [per_device(): key_rows = lax.all_gather(cite_keys, 'paper', axis=0, tiled=True)]
    all_to_all x0 -> x1, waiting for transfers between devices: none -> 66.2 us  [per_device(): lax.all_to_all(jnp.stack([cite_values] * lax.axis_size('paper')), 'paper'...]
    dot_general x10, matrix products: 31.2 us -> 50.4 us  [attend(): jnp.einsum('hts,shd->thd', weights.astype(jnp.bfloat16), head_split(value...]
    dot_general x10, matrix products: 48.6 us -> 64 us  [attend(): jnp.einsum('thd,shd->hts', query_heads, head_split(key_rows, head_count),...]
    all_gather x1, waiting for transfers between devices: 12.6 us -> 0.02 us  [per_device(): key_rows = lax.all_gather(entity_keys, 'type', axis=0, tiled=True)]
    all_gather x1 -> x0, waiting for transfers between devices: 12.5 us -> none  [per_device(): value_rows = lax.all_gather(cite_values, 'paper', axis=0, tiled=True)]
    dynamic_slice x2 -> x18, local copies, waits for them, and re-layouts: 0.42 us -> 10.7 us  [single_block(): part_values = lax.dynamic_slice_in_dim(value_rows, offset, block_rows, 0)]
    all_to_all x0 -> x1, starting transfers between devices: none -> 9.84 us  [per_device(): lax.all_to_all(jnp.stack([cite_values] * lax.axis_size('paper')), 'paper'...]
  transfers between devices with their start and end apart: 4 -> 4, of which waited for: 3 -> 1; matrix products, arithmetic and copies ran while one was open for 40% -> 51% of each run, Pallas kernels for 0% -> 0%
where the time goes in v1:
time: 320 us; the launch traced here: 316 us
  matrix products  136 us (42%)
  waiting for transfers between devices  67 us (21%)
  local copies, waits for them, and re-layouts  58.6 us (18%)
  blocking collectives  23.4 us (7%)
  between operations  14.3 us (4%)
  starting transfers between devices  9.93 us (3%)
  other arithmetic  5.61 us (2%)
    all_to_all x1, waiting for transfers between devices, per_device(): lax.all_to_all(jnp.stack([cite_values] * lax.axis_size('paper')), 'paper'...  66.2 us
    dot_general x10, matrix products, attend(): jnp.einsum('thd,shd->hts', query_heads, head_split(key_rows, head_count),...  64 us
    dot_general x10, matrix products, attend(): jnp.einsum('hts,shd->thd', weights.astype(jnp.bfloat16), head_split(value...  50.4 us
    all_gather x1, blocking collectives, per_device(): kind_ids = lax.all_gather(entity_kinds, 'type', axis=0, tiled=True)  23.4 us
    dynamic_slice x20, local copies, waits for them, and re-layouts, single_block(): part_live = lax.dynamic_slice_in_dim(live_mask, offset, block_rows, 1)  11.8 us
    dynamic_slice x12, local copies, waits for them, and re-layouts, single_block(): part_keys = lax.dynamic_slice_in_dim(key_rows, offset, block_rows, 0)  11.6 us
    dynamic_slice x18, local copies, waits for them, and re-layouts, single_block(): part_values = lax.dynamic_slice_in_dim(value_rows, offset, block_rows, 0)  10.7 us
    all_to_all x1, starting transfers between devices, per_device(): lax.all_to_all(jnp.stack([cite_values] * lax.axis_size('paper')), 'paper'...  9.84 us
  transfers between devices with their start and end apart: 4, of which 1 were waited for; matrix products, arithmetic and copies ran while one was open for 51% of the time, Pallas kernels for 0%

profile of v1, /device:TPU:32, one launch (start us, length us, event | category | flops | bytes accessed | tf_op | source)
XLA Modules:
  0.0 315.6 jit_solution(1327201334112478297)
XLA Ops:
  8.1 1.8 convolution_convert_fusion.7
  12.6 2.9 stack.2
  15.5 9.8 %all-to-all-start = ((bf16[32,128,512]{1,2,0:T(8,128)(2,1)}), bf16[32,128,512]{1,2,0:T(8,128)(2,1)}, u32[]{:S(2)}, u32[]{:S(2)}) async-start(bf16[32,128,512]{1,2,0:T(8,128)(2,1)} %stack.2), calls=%async_computation | async-start | bytes 8388608 | tf_op jit(solution)/shard_map/all_to_all | solution.py:166
  39.3 1.8 convert_element_type.128
  41.1 1.8 broadcast_compare_fusion
  42.9 2.9 copy.163
  47.8 23.4 %all-gather = s32[8,1,128]{2,1,0:T(1,128)S(1)} all-gather(s32[1,1,128]{2,1,0:T(1,128)S(1)} %bitcast.259), channel_id=1, replica_groups=mesh['paper'=32,'type'=8] {'type'}, dimensions={0}, use_global_device_ids=true | all-gather | bytes 4608 | tf_op jit(solution)/shard_map/all_gather | solution.py:177
  73.1 66.2 %all-to-all-done = bf16[32,128,512]{1,2,0:T(8,128)(2,1)} async-done(((bf16[32,128,512]{1,2,0:T(8,128)(2,1)}), bf16[32,128,512]{1,2,0:T(8,128)(2,1)}, u32[]{:S(2)}, u32[]{:S(2)}) %all-to-all-start) | async-done | bytes 4194336 | tf_op jit(solution)/shard_map/all_to_all | solution.py:166
  139.3 6.5 %copy.113 = bf16[32,128,512]{2,1,0:T(8,128)(2,1)} copy(bf16[32,128,512]{1,2,0:T(8,128)(2,1)} %all-to-all-done) | data formatting | bytes 8388608 | tf_op jit(solution)/shard_map/all_to_all | solution.py:166
  146.5 127.6 %while.30 = (s32[]{:T(128)}, f32[512,8,64]{0,2,1:T(8,128)S(1)}, f32[512,8]{0,1:T(8,128)S(1)}, bf16[4096,512]{1,0:T(8,128)(2,1)}, pred[512,4096]{1,0:T(8,128)(4,1...) while((s32[]{:T(128)}, f32[512,8,64]{0,2,1:T(8,128)S(1)}, ...), condition=%wide.region_3.4_spmd, body=%wide.region_1.3_spmd.sunk | while | flops 558104576 | bytes 25297076 | solution.py:118
  149.7 6.4 %fusion.143 = (f32[8,512]{1,0:T(8,128)S(1)}, f32[8,512,512]{2,1,0:T(8,128)}) fusion(f32[8,512]{1,0:T(8,128)S(1)} %dynamic-slice_bitcast_fusion.4, pred[512,512]{0,1:T(8,128)(4,1)S(1)} %copy.171, bf16[512,8,64]{0,2,1:T(8,128)(2,1)S(1)} %bitcast.237, bf16[512,8,64]{0,2,1:T(8,128)(2,1)} %get-tuple-element.541), kind=kOutput, calls=%fused_computation.1.clone.1 | convolution fusion | flops 278917120 | bytes 9732096 | tf_op jit(solution)/shard_map/while/body/eval_jaxpr/thd,shd->hts/dot_general | solution.py:86
  157.4 5.1 %fusion.144 = f32[512,8,64]{0,2,1:T(8,128)S(1)} fusion(f32[512,8,64]{0,2,1:T(8,128)S(1)} %get-tuple-element.524, bf16[512,8,64]{0,2,1:T(8,128)(2,1)S(1)} %bitcast.235, f32[8,512,512]{2,1,0:T(8,128)} %get-tuple-element.497, f32[8,512]{1,0:T(8,128)S(1)} %dynamic-slice_bitcast_fusion.4, pred[512,512]{0,1:T(8,128)(4,1)S(1)} %copy.171), kind=kOutput, calls=%fused_computation.6.clone.1 | convolution fusion | flops 279183360 | bytes 11288576 | tf_op jit(solution)/shard_map/while/body/eval_jaxpr/hts,shd->thd/dot_general | solution.py:96
  165.7 6.4 %fusion.143 = (f32[8,512]{1,0:T(8,128)S(1)}, f32[8,512,512]{2,1,0:T(8,128)}) fusion(f32[8,512]{1,0:T(8,128)S(1)} %dynamic-slice_bitcast_fusion.4, pred[512,512]{0,1:T(8,128)(4,1)S(1)} %copy.171, bf16[512,8,64]{0,2,1:T(8,128)(2,1)S(1)} %bitcast.237, bf16[512,8,64]{0,2,1:T(8,128)(2,1)} %get-tuple-element.541), kind=kOutput, calls=%fused_computation.1.clone.1 | convolution fusion | flops 278917120 | bytes 9732096 | tf_op jit(solution)/shard_map/while/body/eval_jaxpr/thd,shd->hts/dot_general | solution.py:86
  173.4 5.0 %fusion.144 = f32[512,8,64]{0,2,1:T(8,128)S(1)} fusion(f32[512,8,64]{0,2,1:T(8,128)S(1)} %get-tuple-element.524, bf16[512,8,64]{0,2,1:T(8,128)(2,1)S(1)} %bitcast.235, f32[8,512,512]{2,1,0:T(8,128)} %get-tuple-element.497, f32[8,512]{1,0:T(8,128)S(1)} %dynamic-slice_bitcast_fusion.4, pred[512,512]{0,1:T(8,128)(4,1)S(1)} %copy.171), kind=kOutput, calls=%fused_computation.6.clone.1 | convolution fusion | flops 279183360 | bytes 11288576 | tf_op jit(solution)/shard_map/while/body/eval_jaxpr/hts,shd->thd/dot_general | solution.py:96
  181.6 6.4 %fusion.143 = (f32[8,512]{1,0:T(8,128)S(1)}, f32[8,512,512]{2,1,0:T(8,128)}) fusion(f32[8,512]{1,0:T(8,128)S(1)} %dynamic-slice_bitcast_fusion.4, pred[512,512]{0,1:T(8,128)(4,1)S(1)} %copy.171, bf16[512,8,64]{0,2,1:T(8,128)(2,1)S(1)} %bitcast.237, bf16[512,8,64]{0,2,1:T(8,128)(2,1)} %get-tuple-element.541), kind=kOutput, calls=%fused_computation.1.clone.1 | convolution fusion | flops 278917120 | bytes 9732096 | tf_op jit(solution)/shard_map/while/body/eval_jaxpr/thd,shd->hts/dot_general | solution.py:86
  189.3 5.0 %fusion.144 = f32[512,8,64]{0,2,1:T(8,128)S(1)} fusion(f32[512,8,64]{0,2,1:T(8,128)S(1)} %get-tuple-element.524, bf16[512,8,64]{0,2,1:T(8,128)(2,1)S(1)} %bitcast.235, f32[8,512,512]{2,1,0:T(8,128)} %get-tuple-element.497, f32[8,512]{1,0:T(8,128)S(1)} %dynamic-slice_bitcast_fusion.4, pred[512,512]{0,1:T(8,128)(4,1)S(1)} %copy.171), kind=kOutput, calls=%fused_computation.6.clone.1 | convolution fusion | flops 279183360 | bytes 11288576 | tf_op jit(solution)/shard_map/while/body/eval_jaxpr/hts,shd->thd/dot_general | solution.py:96
  197.6 6.4 %fusion.143 = (f32[8,512]{1,0:T(8,128)S(1)}, f32[8,512,512]{2,1,0:T(8,128)}) fusion(f32[8,512]{1,0:T(8,128)S(1)} %dynamic-slice_bitcast_fusion.4, pred[512,512]{0,1:T(8,128)(4,1)S(1)} %copy.171, bf16[512,8,64]{0,2,1:T(8,128)(2,1)S(1)} %bitcast.237, bf16[512,8,64]{0,2,1:T(8,128)(2,1)} %get-tuple-element.541), kind=kOutput, calls=%fused_computation.1.clone.1 | convolution fusion | flops 278917120 | bytes 9732096 | tf_op jit(solution)/shard_map/while/body/eval_jaxpr/thd,shd->hts/dot_general | solution.py:86
  205.3 5.0 %fusion.144 = f32[512,8,64]{0,2,1:T(8,128)S(1)} fusion(f32[512,8,64]{0,2,1:T(8,128)S(1)} %get-tuple-element.524, bf16[512,8,64]{0,2,1:T(8,128)(2,1)S(1)} %bitcast.235, f32[8,512,512]{2,1,0:T(8,128)} %get-tuple-element.497, f32[8,512]{1,0:T(8,128)S(1)} %dynamic-slice_bitcast_fusion.4, pred[512,512]{0,1:T(8,128)(4,1)S(1)} %copy.171), kind=kOutput, calls=%fused_computation.6.clone.1 | convolution fusion | flops 279183360 | bytes 11288576 | tf_op jit(solution)/shard_map/while/body/eval_jaxpr/hts,shd->thd/dot_general | solution.py:96
  213.5 6.4 %fusion.143 = (f32[8,512]{1,0:T(8,128)S(1)}, f32[8,512,512]{2,1,0:T(8,128)}) fusion(f32[8,512]{1,0:T(8,128)S(1)} %dynamic-slice_bitcast_fusion.4, pred[512,512]{0,1:T(8,128)(4,1)S(1)} %copy.171, bf16[512,8,64]{0,2,1:T(8,128)(2,1)S(1)} %bitcast.237, bf16[512,8,64]{0,2,1:T(8,128)(2,1)} %get-tuple-element.541), kind=kOutput, calls=%fused_computation.1.clone.1 | convolution fusion | flops 278917120 | bytes 9732096 | tf_op jit(solution)/shard_map/while/body/eval_jaxpr/thd,shd->hts/dot_general | solution.py:86
  221.2 5.0 %fusion.144 = f32[512,8,64]{0,2,1:T(8,128)S(1)} fusion(f32[512,8,64]{0,2,1:T(8,128)S(1)} %get-tuple-element.524, bf16[512,8,64]{0,2,1:T(8,128)(2,1)S(1)} %bitcast.235, f32[8,512,512]{2,1,0:T(8,128)} %get-tuple-element.497, f32[8,512]{1,0:T(8,128)S(1)} %dynamic-slice_bitcast_fusion.4, pred[512,512]{0,1:T(8,128)(4,1)S(1)} %copy.171), kind=kOutput, calls=%fused_computation.6.clone.1 | convolution fusion | flops 279183360 | bytes 11288576 | tf_op jit(solution)/shard_map/while/body/eval_jaxpr/hts,shd->thd/dot_general | solution.py:96
  229.5 6.4 %fusion.143 = (f32[8,512]{1,0:T(8,128)S(1)}, f32[8,512,512]{2,1,0:T(8,128)}) fusion(f32[8,512]{1,0:T(8,128)S(1)} %dynamic-slice_bitcast_fusion.4, pred[512,512]{0,1:T(8,128)(4,1)S(1)} %copy.171, bf16[512,8,64]{0,2,1:T(8,128)(2,1)S(1)} %bitcast.237, bf16[512,8,64]{0,2,1:T(8,128)(2,1)} %get-tuple-element.541), kind=kOutput, calls=%fused_computation.1.clone.1 | convolution fusion | flops 278917120 | bytes 9732096 | tf_op jit(solution)/shard_map/while/body/eval_jaxpr/thd,shd->hts/dot_general | solution.py:86
  237.2 5.0 %fusion.144 = f32[512,8,64]{0,2,1:T(8,128)S(1)} fusion(f32[512,8,64]{0,2,1:T(8,128)S(1)} %get-tuple-element.524, bf16[512,8,64]{0,2,1:T(8,128)(2,1)S(1)} %bitcast.235, f32[8,512,512]{2,1,0:T(8,128)} %get-tuple-element.497, f32[8,512]{1,0:T(8,128)S(1)} %dynamic-slice_bitcast_fusion.4, pred[512,512]{0,1:T(8,128)(4,1)S(1)} %copy.171), kind=kOutput, calls=%fused_computation.6.clone.1 | convolution fusion | flops 279183360 | bytes 11288576 | tf_op jit(solution)/shard_map/while/body/eval_jaxpr/hts,shd->thd/dot_general | solution.py:96
  245.4 6.4 %fusion.143 = (f32[8,512]{1,0:T(8,128)S(1)}, f32[8,512,512]{2,1,0:T(8,128)}) fusion(f32[8,512]{1,0:T(8,128)S(1)} %dynamic-slice_bitcast_fusion.4, pred[512,512]{0,1:T(8,128)(4,1)S(1)} %copy.171, bf16[512,8,64]{0,2,1:T(8,128)(2,1)S(1)} %bitcast.237, bf16[512,8,64]{0,2,1:T(8,128)(2,1)} %get-tuple-element.541), kind=kOutput, calls=%fused_computation.1.clone.1 | convolution fusion | flops 278917120 | bytes 9732096 | tf_op jit(solution)/shard_map/while/body/eval_jaxpr/thd,shd->hts/dot_general | solution.py:86
  253.1 5.0 %fusion.144 = f32[512,8,64]{0,2,1:T(8,128)S(1)} fusion(f32[512,8,64]{0,2,1:T(8,128)S(1)} %get-tuple-element.524, bf16[512,8,64]{0,2,1:T(8,128)(2,1)S(1)} %bitcast.235, f32[8,512,512]{2,1,0:T(8,128)} %get-tuple-element.497, f32[8,512]{1,0:T(8,128)S(1)} %dynamic-slice_bitcast_fusion.4, pred[512,512]{0,1:T(8,128)(4,1)S(1)} %copy.171), kind=kOutput, calls=%fused_computation.6.clone.1 | convolution fusion | flops 279183360 | bytes 11288576 | tf_op jit(solution)/shard_map/while/body/eval_jaxpr/hts,shd->thd/dot_general | solution.py:96
  261.4 6.4 %fusion.143 = (f32[8,512]{1,0:T(8,128)S(1)}, f32[8,512,512]{2,1,0:T(8,128)}) fusion(f32[8,512]{1,0:T(8,128)S(1)} %dynamic-slice_bitcast_fusion.4, pred[512,512]{0,1:T(8,128)(4,1)S(1)} %copy.171, bf16[512,8,64]{0,2,1:T(8,128)(2,1)S(1)} %bitcast.237, bf16[512,8,64]{0,2,1:T(8,128)(2,1)} %get-tuple-element.541), kind=kOutput, calls=%fused_computation.1.clone.1 | convolution fusion | flops 278917120 | bytes 9732096 | tf_op jit(solution)/shard_map/while/body/eval_jaxpr/thd,shd->hts/dot_general | solution.py:86
  269.1 5.0 %fusion.144 = f32[512,8,64]{0,2,1:T(8,128)S(1)} fusion(f32[512,8,64]{0,2,1:T(8,128)S(1)} %get-tuple-element.524, bf16[512,8,64]{0,2,1:T(8,128)(2,1)S(1)} %bitcast.235, f32[8,512,512]{2,1,0:T(8,128)} %get-tuple-element.497, f32[8,512]{1,0:T(8,128)S(1)} %dynamic-slice_bitcast_fusion.4, pred[512,512]{0,1:T(8,128)(4,1)S(1)} %copy.171), kind=kOutput, calls=%fused_computation.6.clone.1 | convolution fusion | flops 279183360 | bytes 11288576 | tf_op jit(solution)/shard_map/while/body/eval_jaxpr/hts,shd->thd/dot_general | solution.py:96
  274.2 29.6 %while.31 = (s32[]{:T(128)}, f32[512,8,64]{0,2,1:T(8,128)S(1)}, f32[512,8]{0,1:T(8,128)S(1)}, bf16[1024,512]{1,0:T(8,128)(2,1)}, pred[512,1024]{1,0:T(8,128)(4,1...) while((s32[]{:T(128)}, f32[512,8,64]{0,2,1:T(8,128)S(1)}, ...), condition=%wide.region_6.7_spmd, body=%wide.region_4.6_spmd.sunk | while | flops 558104576 | bytes 34734312 | solution.py:118
  277.2 6.5 %fusion.149 = (f32[8,512]{1,0:T(8,128)S(1)}, f32[8,512,512]{2,1,0:T(8,128)}) fusion(f32[8,512]{1,0:T(8,128)S(1)} %dynamic-slice_bitcast_fusion.5, pred[512,512]{0,1:T(8,128)(4,1)S(1)} %copy.173, bf16[512,8,64]{0,2,1:T(8,128)(2,1)S(1)} %bitcast.234, bf16[512,8,64]{0,2,1:T(8,128)(2,1)} %get-tuple-element.577), kind=kOutput, calls=%fused_computation.16.clone.1 | convolution fusion | flops 278917120 | bytes 9732096 | tf_op jit(solution)/shard_map/while/body/eval_jaxpr/thd,shd->hts/dot_general | solution.py:86
  283.9 5.0 %fusion.150 = f32[512,8,64]{0,2,1:T(8,128)S(1)} fusion(f32[512,8,64]{0,2,1:T(8,128)S(1)} %copy-done.2, bf16[512,8,64]{0,2,1:T(8,128)(2,1)S(1)} %bitcast.236, f32[8,512,512]{2,1,0:T(8,128)} %get-tuple-element.509, f32[8,512]{1,0:T(8,128)S(1)} %dynamic-slice_bitcast_fusion.5, pred[512,512]{0,1:T(8,128)(4,1)S(1)} %copy.173), kind=kOutput, calls=%fused_computation.21.clone.1 | convolution fusion | flops 279183360 | bytes 11288576 | tf_op jit(solution)/shard_map/while/body/eval_jaxpr/hts,shd->thd/dot_general | solution.py:96
  292.0 6.5 %fusion.149 = (f32[8,512]{1,0:T(8,128)S(1)}, f32[8,512,512]{2,1,0:T(8,128)}) fusion(f32[8,512]{1,0:T(8,128)S(1)} %dynamic-slice_bitcast_fusion.5, pred[512,512]{0,1:T(8,128)(4,1)S(1)} %copy.173, bf16[512,8,64]{0,2,1:T(8,128)(2,1)S(1)} %bitcast.234, bf16[512,8,64]{0,2,1:T(8,128)(2,1)} %get-tuple-element.577), kind=kOutput, calls=%fused_computation.16.clone.1 | convolution fusion | flops 278917120 | bytes 9732096 | tf_op jit(solution)/shard_map/while/body/eval_jaxpr/thd,shd->hts/dot_general | solution.py:86
  298.7 5.0 %fusion.150 = f32[512,8,64]{0,2,1:T(8,128)S(1)} fusion(f32[512,8,64]{0,2,1:T(8,128)S(1)} %copy-done.2, bf16[512,8,64]{0,2,1:T(8,128)(2,1)S(1)} %bitcast.236, f32[8,512,512]{2,1,0:T(8,128)} %get-tuple-element.509, f32[8,512]{1,0:T(8,128)S(1)} %dynamic-slice_bitcast_fusion.5, pred[512,512]{0,1:T(8,128)(4,1)S(1)} %copy.173), kind=kOutput, calls=%fused_computation.21.clone.1 | convolution fusion | flops 279183360 | bytes 11288576 | tf_op jit(solution)/shard_map/while/body/eval_jaxpr/hts,shd->thd/dot_general | solution.py:96
  303.8 2.4 fusion.40
  (161 shorter events, 66.8 us)
Async XLA Ops:
  6.5 299.6 %copy-start = (bf16[512,512]{1,0:T(8,128)(2,1)S(1)}, bf16[512,512]{1,0:T(8,128)(2,1)}, u32[]{:S(2)}) copy-start(bf16[512,512]{1,0:T(8,128)(2,1)} %param.33) | copy-start | bytes 1572868
  6.5 18.9 %copy-start.12 = (s32[128]{0:T(128)S(1)}, s32[128]{0:T(128)}, u32[]{:S(2)}) copy-start(s32[128]{0:T(128)} %param.26) | copy-start | bytes 1540
  6.5 19.0 %copy-start.13 = (bf16[128,512]{1,0:T(8,128)(2,1)S(1)}, bf16[128,512]{1,0:T(8,128)(2,1)}, u32[]{:S(2)}) copy-start(bf16[128,512]{1,0:T(8,128)(2,1)} %param.25) | copy-start | bytes 393220
  6.5 139.3 %all-gather.5.cloned.1.call-start = ((), (), s32[]{:S(2)}) async-start(), calls=%async_computation.1 | async-start | bytes 4325376 | tf_op jit(solution)/shard_map/all_gather | solution.py:164
  8.1 20.1 %copy-start.7 = (bf16[4,8,64,64]{3,2,1,0:T(8,128)(2,1)S(1)}, bf16[4,8,64,64]{3,2,1,0:T(8,128)(2,1)}, u32[]{:S(2)}) copy-start(bf16[4,8,64,64]{3,2,1,0:T(8,128)(2,1)} %param.31) | copy-start | bytes 786436
  12.6 19.0 %copy-start.5 = (bf16[4,8,64,64]{3,2,1,0:T(8,128)(2,1)S(1)}, bf16[4,8,64,64]{3,2,1,0:T(8,128)(2,1)}, u32[]{:S(2)}) copy-start(bf16[4,8,64,64]{3,2,1,0:T(8,128)(2,1)} %param.30) | copy-start | bytes 786436
  15.5 18.4 %copy-start.3 = (bf16[512,512]{1,0:T(8,128)(2,1)S(1)}, bf16[512,512]{1,0:T(8,128)(2,1)}, u32[]{:S(2)}) copy-start(bf16[512,512]{1,0:T(8,128)(2,1)} %param.23) | copy-start | bytes 1572868
  15.5 20.9 %copy-start.4 = (bf16[512,512]{1,0:T(8,128)(2,1)S(1)}, bf16[512,512]{1,0:T(8,128)(2,1)}, u32[]{:S(2)}) copy-start(bf16[512,512]{1,0:T(8,128)(2,1)} %param.27) | copy-start | bytes 1572868
  15.5 123.8 %all-to-all-start = ((bf16[32,128,512]{1,2,0:T(8,128)(2,1)}), bf16[32,128,512]{1,2,0:T(8,128)(2,1)}, u32[]{:S(2)}, u32[]{:S(2)}) async-start(bf16[32,128,512]{1,2,0:T(8,128)(2,1)} %stack.2), calls=%async_computation | async-start | bytes 8388608 | tf_op jit(solution)/shard_map/all_to_all | solution.py:166
  25.4 13.8 %copy-start.10 = (f32[4,8]{1,0:T(4,128)S(1)}, f32[4,8]{1,0:T(4,128)}, u32[]{:S(2)}) copy-start(f32[4,8]{1,0:T(4,128)} %param.32) | copy-start | bytes 388
  25.4 15.7 %copy-start.9 = (s32[4,8]{1,0:T(4,128)S(1)}, s32[4,8]{1,0:T(4,128)}, u32[]{:S(2)}) copy-start(s32[4,8]{1,0:T(4,128)} %param.38) | copy-start | bytes 388
  25.4 15.7 %copy-start.14 = (s32[4,8]{1,0:T(4,128)S(1)}, s32[4,8]{1,0:T(4,128)}, u32[]{:S(2)}) copy-start(s32[4,8]{1,0:T(4,128)} %param.37) | copy-start | bytes 388
  25.4 248.7 %all-gather.7.cloned.1.call-start = ((), (), s32[]{:S(2)}) async-start(), calls=%async_computation.2 | async-start | bytes 1179648 | tf_op jit(solution)/shard_map/all_gather | solution.py:176
  33.1 241.0 %all-gather.9.cloned.1.call-start = ((), (), s32[]{:S(2)}) async-start(), calls=%async_computation.3 | async-start | bytes 1179648 | tf_op jit(solution)/shard_map/all_gather | solution.py:175
  41.1 4.7 %copy-start.6 = (s32[4,2,128,128]{3,2,1,0:T(8,128)S(1)}, s32[4,2,128,128]{3,2,1,0:T(8,128)}, u32[]{:S(2)}) copy-start(s32[4,2,128,128]{3,2,1,0:T(8,128)} %param.39) | copy-start | bytes 1572868
  41.1 4.8 %copy-start.11 = (s32[4,2]{0,1:T(2,128)S(1)}, s32[4,2]{0,1:T(2,128)}, u32[]{:S(2)}) copy-start(s32[4,2]{0,1:T(2,128)} %param.40) | copy-start | bytes 100
  41.1 4.9 %copy-start.15 = (s32[4,2]{0,1:T(2,128)S(1)}, s32[4,2]{0,1:T(2,128)}, u32[]{:S(2)}) copy-start(s32[4,2]{0,1:T(2,128)} %param.41) | copy-start | bytes 100
  274.2 33.8 %copy-start.8 = (f32[512]{0:T(512)S(1)}, f32[512]{0:T(512)}, u32[]{:S(2)}) copy-start(f32[512]{0:T(512)} %param.35) | copy-start | bytes 6148
  274.2 1.1 copy-start.1
  277.2 6.7 %copy-start.2 = (f32[512,8,64]{0,2,1:T(8,128)S(1)}, f32[512,8,64]{0,2,1:T(8,128)}, u32[]{:S(2)}) copy-start(f32[512,8,64]{0,2,1:T(8,128)} %copy-done.1) | copy-start | bytes 3145732 | tf_op jit(solution)/shard_map/while
  289.0 1.1 copy-start.1
  292.0 6.7 %copy-start.2 = (f32[512,8,64]{0,2,1:T(8,128)S(1)}, f32[512,8,64]{0,2,1:T(8,128)}, u32[]{:S(2)}) copy-start(f32[512,8,64]{0,2,1:T(8,128)} %copy-done.1) | copy-start | bytes 3145732 | tf_op jit(solution)/shard_map/while
Sparse Core Ops, SparseCore 0:
  10.1 133.3 all-gather.4
  146.1 52.4 all-gather.6
  201.2 50.2 all-gather.8
